TPU v7x, 32 devices: a whole 2x2x4 slice. The times are simulated.
32 devices in a mesh: groups: 2 (over x), frame: 16 (over z, y, core).
Axes of the slice: x: 2, y: 2, z: 4, core: 2. Of those that a mesh axis runs over, the one named last changes fastest.
Arguments:
- frames_in: bfloat16 [32, 256, 2240], P(('groups', 'frame')), parts along dimension 0, may hold values from -16 to 16
- qkv_weight: bfloat16 [3, 2240, 1280], P(None, None, 'frame'), may hold values from -0.125 to 0.125
Outputs:
- attended: bfloat16 [32, 256, 1280], P(('groups', 'frame')), parts along dimension 0
There are 2 independent parts, one for each index of `groups`. A program takes and returns all parts, laid end to end along the dimension named above; an argument that names none is the same for every part. Nothing has to cross between parts.
All inputs are finite; a program needn't handle non-finite values.
Results may differ from a plain program's by a relative error of at most 0.0039.
Values may be sent and summed in bfloat16 or wider, within the bound.
A program may use at most 128 MiB of HBM per device.

v0:
```python
import jax
import jax.numpy as jnp
from jax import lax
from jax.sharding import PartitionSpec as P

HEAD_DIM = 32
HEADS = 40
EPSILON = 1e-06


def entering(shard, axis, join, neutral):
    place = lax.axis_index(axis)
    gathered = jax.tree.map(
        lambda a, kind: lax.all_gather(a.astype(kind), axis), shard, (jnp.bfloat16, jnp.bfloat16)
    )
    state = jax.tree.map(lambda a, e: jnp.zeros_like(a) + jnp.asarray(e, a.dtype), shard, neutral)

    def one(hop, state):
        return join(
            state,
            jax.tree.map(
                lambda a, own: lax.dynamic_index_in_dim(a, hop, 0, False).astype(own.dtype),
                gathered,
                shard,
            ),
        )

    return lax.fori_loop(0, place, one, state)


def add_pair(earlier, later):
    return (earlier[0] + later[0], earlier[1] + later[1])


def carry_states(key_rows, value_rows):
    count = key_rows.shape[0]
    feature_k = jax.nn.relu(key_rows).reshape(count, HEADS, HEAD_DIM)
    values = value_rows.reshape(count, HEADS, HEAD_DIM)
    local_state = jnp.einsum("thi,thj->hij", feature_k, values, preferred_element_type=jnp.float32)
    local_keys = jnp.sum(feature_k.astype(jnp.float32), axis=0)
    prior_state, prior_keys = entering(
        (local_state, local_keys),
        "frame",
        add_pair,
        (jnp.zeros_like(local_state), jnp.zeros_like(local_keys)),
    )
    return (local_state, local_keys, prior_state, prior_keys)


def apply_state(feature_q, state, key_sum):
    numer = jnp.einsum("thi,hij->thj", feature_q, state, precision=lax.Precision.HIGHEST)
    denom = jnp.einsum("thi,hi->th", feature_q, key_sum, precision=lax.Precision.HIGHEST)
    return (numer, denom)


def shards(frames_in, qkv_weight):
    tokens = frames_in[0]
    count = tokens.shape[0]
    weights_all = lax.all_gather(qkv_weight, "frame", axis=2, tiled=True)
    projected = jnp.einsum("td,sdc->stc", tokens, weights_all, preferred_element_type=jnp.float32)
    queries = projected[0]
    key_rows = projected[1].astype(jnp.bfloat16)
    value_rows = projected[2].astype(jnp.bfloat16)
    local_state, local_keys, prior_state, prior_keys = carry_states(key_rows, value_rows)
    feature_q = jax.nn.relu(queries).reshape(count, HEADS, HEAD_DIM)
    own_numer, own_denom = apply_state(feature_q, local_state, local_keys)
    past_numer, past_denom = apply_state(feature_q, prior_state, prior_keys)
    numer = past_numer + own_numer
    denom = past_denom + own_denom
    attended = (numer / (denom[:, :, None] + EPSILON)).astype(jnp.bfloat16)
    return attended.reshape(1, count, HEADS * HEAD_DIM)


def solution(mesh):
    placed = (P(("groups", "frame"), None, None), P(None, None, "frame"))
    return jax.shard_map(
        shards,
        mesh=mesh,
        in_specs=placed,
        out_specs=P(("groups", "frame"), None, None),
        check_vma=False,
    )
```

profile of v0, /device:TPU:29, one launch (start us, length us, event | category | flops | bytes accessed | tf_op | source)
XLA Modules:
  0.0 198.7 jit_solution(12941034522131766999)
XLA Ops:
  6.5 0.0 copy-start
  6.5 0.0 all-gather.4.cloned.1.call-start
  6.5 0.7 all-gather.4.cloned.1.call-update
  7.3 0.0 all-gather.6.cloned.1.call-start
  7.3 95.5 %all-gather.4.cloned.1.call-done = bf16[3,2240,1280]{1,2,0:T(8,128)(2,1)} async-done(((bf16[3,2240,80]{1,2,0:T(8,128)(2,1)}), bf16[3,2240,1280]{1,2,0:T(8,128)(2,1)}) %all-gather.4.cloned.1.call-update) | async-done | bytes 17203216 | tf_op jit(solution)/shard_map/all_gather | solution.py:59
  102.8 0.0 copy-done
  102.8 8.5 %convolution_bitcast_fusion = f32[3,256,1280]{1,2,0:T(8,128)S(1)} fusion(bf16[3,2240,1280]{1,2,0:T(8,128)(2,1)} %all-gather.4.cloned.1.call-done, bf16[1,256,2240]{1,2,0:T(8,128)(2,1)S(1)} %copy-done), kind=kOutput, calls=%fused_computation.3 | convolution fusion | flops 4404019200 | bytes 22282240 | tf_op jit(solution)/shard_map/td,sdc->stc/dot_general | solution.py:60
  111.3 0.3 convert_reduce_fusion
  111.6 0.1 slice.21
  111.6 1.3 fusion.8
  112.9 0.0 all-gather.6.cloned.1.call-update
  113.0 0.1 reshape.41
  113.0 0.1 convert_element_type.51
  113.1 0.1 copy.9
  113.2 17.0 %all_gather.16 = bf16[16,40,32]{1,2,0:T(8,128)(2,1)S(1)} all-gather(bf16[1,40,32]{1,2,0:T(8,128)(2,1)S(1)} %copy.9), channel_id=1, replica_groups=mesh['groups'=2,'frame'=16] {'frame'}, dimensions={0}, use_global_device_ids=true | all-gather | bytes 43520 | tf_op jit(solution)/shard_map/all_gather | solution.py:14
  130.2 0.8 fusion.11
  130.9 37.0 %all-gather.6.cloned.1.call-done = bf16[640,32,32]{2,1,0:T(8,128)(2,1)} async-done(((bf16[40,32,32]{2,1,0:T(8,128)(2,1)}), bf16[640,32,32]{2,1,0:T(8,128)(2,1)}) %all-gather.6.cloned.1.call-update) | async-done | bytes 1310736 | tf_op jit(solution)/shard_map/all_gather | solution.py:14
  168.0 0.1 broadcast_in_dim.7
  168.1 19.2 %while.12 = (s32[]{:T(128)}, f32[40,32,32]{2,1,0:T(8,128)S(1)}, f32[40,32]{1,0:T(8,128)S(1)}, s32[]{:T(128)}, bf16[16,40,32,32]{3,2,1,0:T(8,128)(2,1)}, /*index=...) while((s32[]{:T(128)}, f32[40,32,32]{2,1,0:T(8,128)S(1)}, f32[40,32]{1,0:T(8,128)S(1)}, ...), condition=%wide.region_2.3_spmd, body=%wide.region_1.2_spmd.sunk | while | flops 84485 | bytes 432775 | solution.py:28
  168.1 1.1 convert_add_fusion.4
  169.2 0.1 copy.24
  169.4 1.1 convert_add_fusion.4
  170.5 0.1 copy.24
  170.6 1.1 convert_add_fusion.4
  171.8 0.1 copy.24
  171.9 1.1 convert_add_fusion.4
  173.1 0.1 copy.24
  173.2 1.1 convert_add_fusion.4
  174.4 0.1 copy.24
  174.5 1.1 convert_add_fusion.4
  175.6 0.1 copy.24
  175.8 1.1 convert_add_fusion.4
  176.9 0.1 copy.24
  177.0 1.1 convert_add_fusion.4
  178.2 0.1 copy.24
  178.3 1.1 convert_add_fusion.4
  179.5 0.1 copy.24
  179.6 1.1 convert_add_fusion.4
  180.8 0.1 copy.24
  180.9 1.1 convert_add_fusion.4
  182.0 0.1 copy.24
  182.2 1.1 convert_add_fusion.4
  183.3 0.1 copy.24
  183.4 1.1 convert_add_fusion.4
  184.6 0.1 copy.24
  184.7 1.1 convert_add_fusion.4
  185.9 0.1 copy.24
  186.0 1.1 convert_add_fusion.4
  187.2 0.1 copy.24
  187.3 0.8 fusion.10
  188.0 0.0 copy-start.1
  188.0 1.3 fusion.9
  189.4 0.0 copy-done.1
  189.4 1.4 fusion.2
  190.8 1.1 copy.13
  (33 shorter events, 0.3 us)
Async XLA Ops:
  6.5 96.2 %copy-start = (bf16[1,256,2240]{1,2,0:T(8,128)(2,1)S(1)}, bf16[1,256,2240]{1,2,0:T(8,128)(2,1)}, u32[]{:S(2)}) copy-start(bf16[1,256,2240]{1,2,0:T(8,128)(2,1)} %param.4) | copy-start | bytes 3440644
  6.5 96.2 %all-gather.4.cloned.1.call-start = ((), (), s32[]{:S(2)}) async-start(), calls=%async_computation | async-start | bytes 18800640 | tf_op jit(solution)/shard_map/all_gather | solution.py:59
  7.3 160.7 %all-gather.6.cloned.1.call-start = ((), (), s32[]{:S(2)}) async-start(), calls=%async_computation.1 | async-start | bytes 5570560 | tf_op jit(solution)/shard_map/all_gather | solution.py:14
  188.0 1.4 copy-start.1
Sparse Core Ops, SparseCore 0:
  8.9 93.8 all-gather.3
  113.1 54.8 all-gather.5
where the time goes:
time: 199 us
  waiting for transfers between devices  133 us (67%)
  other arithmetic  17.4 us (9%)
  blocking collectives  17 us (9%)
  matrix products  14 us (7%)
  between operations  13.5 us (7%)
  local copies, waits for them, and re-layouts  2.92 us (1%)
    all_gather x1, waiting for transfers between devices, shards(): weights_all = lax.all_gather(qkv_weight, 'frame', axis=2, tiled=True)  95.5 us
    all_gather x1, waiting for transfers between devices, entering(): lax.all_gather(a.astype(kind), axis)  37 us
    add x30, other arithmetic, add_pair(): return (earlier[0] + later[0], earlier[1] + later[1])  17.2 us
    all_gather x1, blocking collectives, entering(): lax.all_gather(a.astype(kind), axis)  17 us
    dot_general x1, matrix products, shards(): jnp.einsum('td,sdc->stc', tokens, weights_all, preferred_element_type=jnp...  8.53 us
  transfers between devices with their start and end apart: 2, of which 2 were waited for; matrix products, arithmetic and copies ran while one was open for 1% of the time, Pallas kernels for 0%

commit v1 on v0

--- a/solution.py
+++ b/solution.py
@@ -6,6 +6,35 @@
 HEAD_DIM = 32
 HEADS = 40
 EPSILON = 1e-06
+
+
+def knots_play(row_data, dim_at):
+    row_data = jnp.moveaxis(row_data, 0, dim_at)
+    low = row_data.shape
+    return row_data.reshape(*low[:dim_at], low[dim_at] * low[dim_at + 1], *low[dim_at + 2 :])
+
+
+def _deliver_thing(vector, bus_axis, dim_k, mine_x, k_dim):
+    right_arr = jax.lax.axis_index(bus_axis)
+    after = jax.lax.axis_size(bus_axis)
+    kept_arr, d_next, high = (after, right_arr, vector.shape[dim_k])
+    kept_rows = [(tick, (tick + 1) % kept_arr) for tick in range(kept_arr)]
+    answer = kept_arr // 2
+    outcome_arr = {}
+    mat_out = base_arr = vector
+    tray = [(tick, (tick - 1) % kept_arr) for tick in range(kept_arr)]
+    for to_i in range(answer + 1):
+        b_next = jax.lax.ppermute(mat_out, bus_axis, kept_rows) if to_i < answer else None
+        t_next = (
+            jax.lax.ppermute(base_arr, bus_axis, tray) if to_i < kept_arr - answer - 1 else None
+        )
+        outcome_arr[-to_i] = mine_x(mat_out, (d_next - to_i) % kept_arr * high)
+        if 0 < to_i < kept_arr - answer:
+            outcome_arr[to_i] = mine_x(base_arr, (d_next + to_i) % kept_arr * high)
+        mat_out, base_arr = (b_next, t_next)
+    outcome_arr = jnp.stack([outcome_arr[s] for s in sorted(outcome_arr)], axis=0)
+    outcome_arr = outcome_arr[(jnp.arange(kept_arr) - d_next + answer) % kept_arr]
+    return knots_play(outcome_arr, k_dim)
 
 
 def entering(shard, axis, join, neutral):
@@ -56,8 +85,15 @@
 def shards(frames_in, qkv_weight):
     tokens = frames_in[0]
     count = tokens.shape[0]
-    weights_all = lax.all_gather(qkv_weight, "frame", axis=2, tiled=True)
-    projected = jnp.einsum("td,sdc->stc", tokens, weights_all, preferred_element_type=jnp.float32)
+    projected = _deliver_thing(
+        qkv_weight,
+        "frame",
+        2,
+        lambda part, offset: jnp.einsum(
+            "td,sdc->stc", tokens, part, preferred_element_type=jnp.float32
+        ),
+        2,
+    )
     queries = projected[0]
     key_rows = projected[1].astype(jnp.bfloat16)
     value_rows = projected[2].astype(jnp.bfloat16)

time: 199 us -> 324 us (1.63)
  starting transfers between devices: 0.04 us -> 140 us
  waiting for transfers between devices: 133 us -> 77.2 us
  matrix products: 14 us -> 29.1 us
  blocking collectives: 17 us -> 32.1 us
  local copies, waits for them, and re-layouts: 2.92 us -> 10.7 us
    ppermute x0 -> x15, starting transfers between devices: none -> 140 us  [the longest x7 130 us: _deliver_thing(): jax.lax.ppermute(base_arr, bus_axis, tray)]
    all_gather x1 -> x0, waiting for transfers between devices: 95.5 us -> none  [shards(): weights_all = lax.all_gather(qkv_weight, 'frame', axis=2, tiled=True)]
    ppermute x0 -> x15, waiting for transfers between devices: none -> 40.2 us  [the longest x8 25 us: _deliver_thing(): jax.lax.ppermute(mat_out, bus_axis, kept_rows)]
    dot_general x1 -> x16, matrix products: 8.53 us -> 23.7 us  [shards(): jnp.einsum('td,sdc->stc', tokens, part, preferred_element_type=jnp.float32)]
    all_gather x1, blocking collectives: 17 us -> 32.1 us  [entering(): lax.all_gather(a.astype(kind), axis)]
    gather x0 -> x1, local copies, waits for them, and re-layouts: none -> 4.81 us  [_deliver_thing(): outcome_arr[(jnp.arange(kept_arr) - d_next + answer) % kept_arr]]
  transfers between devices with their start and end apart: 2 -> 16, of which waited for: 2 -> 9; matrix products, arithmetic and copies ran while one was open for 1% -> 7% of each run, Pallas kernels for 0% -> 0%
where the time goes in v1:
time: 324 us; the launch traced here: 323 us
  starting transfers between devices  140 us (43%)
  waiting for transfers between devices  77.2 us (24%)
  blocking collectives  32.1 us (10%)
  matrix products  29.1 us (9%)
  other arithmetic  19.3 us (6%)
  between operations  13.6 us (4%)
  local copies, waits for them, and re-layouts  10.7 us (3%)
    ppermute x7, starting transfers between devices, _deliver_thing(): jax.lax.ppermute(base_arr, bus_axis, tray)  130 us
    all_gather x1, waiting for transfers between devices, entering(): lax.all_gather(a.astype(kind), axis)  37 us
    all_gather x1, blocking collectives, entering(): lax.all_gather(a.astype(kind), axis)  32.1 us
    ppermute x8, waiting for transfers between devices, _deliver_thing(): jax.lax.ppermute(mat_out, bus_axis, kept_rows)  25 us
    dot_general x16, matrix products, shards(): jnp.einsum('td,sdc->stc', tokens, part, preferred_element_type=jnp.float32)  23.7 us
    add x30, other arithmetic, add_pair(): return (earlier[0] + later[0], earlier[1] + later[1])  17.2 us
    ppermute x7, waiting for transfers between devices, _deliver_thing(): jax.lax.ppermute(base_arr, bus_axis, tray)  15.1 us
    ppermute x8, starting transfers between devices, _deliver_thing(): jax.lax.ppermute(mat_out, bus_axis, kept_rows)  10.5 us
  transfers between devices with their start and end apart: 16, of which 9 were waited for; matrix products, arithmetic and copies ran while one was open for 7% of the time, Pallas kernels for 0%

profile of v1, /device:TPU:29, one launch (start us, length us, event | category | flops | bytes accessed | tf_op | source)
XLA Modules:
  0.0 322.8 jit_solution(1313676111004343440)
XLA Ops:
  6.5 12.7 %collective-permute-done = bf16[3,2240,80]{1,2,0:T(8,128)(2,1)S(1)} collective-permute-done((bf16[3,2240,80]{1,2,0:T(8,128)(2,1)}, bf16[3,2240,80]{1,2,0:T(8,128)(2,1)S(1)}, u32[]{:S(2)}, u32[]{:S(2)}) %collective-permute-start) | collective-permute-done | bytes 1075232 | tf_op jit(solution)/shard_map/ppermute | solution.py:27
  19.2 5.1 %collective-permute-start.1 = (bf16[3,2240,80]{1,2,0:T(8,128)(2,1)S(1)}, bf16[3,2240,80]{1,2,0:T(8,128)(2,1)S(1)}, u32[]{:S(2)}, u32[]{:S(2)}) collective-permute-start(bf16[3,2240,80]{1,2,0:T(8,128)(2,1)S(1)} %collective-permute-done), channel_id=1, source_target_pairs={{0,1},{1,2},{2,3},{3,4},{4,5},{5,6},{6,7},{7,8},{8,9},{9,10},{10,1... | collective-permute-start | bytes 3225608 | tf_op jit(solution)/shard_map/ppermute | solution.py:27
  24.3 12.4 %collective-permute-done.1 = bf16[3,2240,80]{1,2,0:T(8,128)(2,1)S(1)} collective-permute-done((bf16[3,2240,80]{1,2,0:T(8,128)(2,1)S(1)}, bf16[3,2240,80]{1,2,0:T(8,128)(2,1)S(1)}, u32[]{:S(2)}, u32[]{:S(2)}) %collective-permute-start.1) | collective-permute-done | bytes 1075232 | tf_op jit(solution)/shard_map/ppermute | solution.py:27
  36.6 5.3 %collective-permute-start.2 = (bf16[3,2240,80]{1,2,0:T(8,128)(2,1)S(1)}, bf16[3,2240,80]{1,2,0:T(8,128)(2,1)S(1)}, u32[]{:S(2)}, u32[]{:S(2)}) collective-permute-start(bf16[3,2240,80]{1,2,0:T(8,128)(2,1)S(1)} %collective-permute-done.1), channel_id=1, source_target_pairs={{0,1},{1,2},{2,3},{3,4},{4,5},{5,6},{6,7},{7,8},{8,9},{9,10},{10,1... | collective-permute-start | bytes 3225608 | tf_op jit(solution)/shard_map/ppermute | solution.py:27
  41.9 0.2 collective-permute-done.8
  42.1 18.6 %collective-permute-start.9 = (bf16[3,2240,80]{1,2,0:T(8,128)(2,1)S(1)}, bf16[3,2240,80]{1,2,0:T(8,128)(2,1)S(1)}, u32[]{:S(2)}, u32[]{:S(2)}) collective-permute-start(bf16[3,2240,80]{1,2,0:T(8,128)(2,1)S(1)} %collective-permute-done.8), channel_id=1, source_target_pairs={{0,15},{1,0},{2,1},{3,2},{4,3},{5,4},{6,5},{7,6},{8,7},{9,8},{10,9... | collective-permute-start | bytes 3225608 | tf_op jit(solution)/shard_map/ppermute | solution.py:29
  60.7 2.4 collective-permute-done.9
  63.1 22.1 %collective-permute-start.10 = (bf16[3,2240,80]{1,2,0:T(8,128)(2,1)S(1)}, bf16[3,2240,80]{1,2,0:T(8,128)(2,1)S(1)}, u32[]{:S(2)}, u32[]{:S(2)}) collective-permute-start(bf16[3,2240,80]{1,2,0:T(8,128)(2,1)S(1)} %collective-permute-done.9), channel_id=1, source_target_pairs={{0,15},{1,0},{2,1},{3,2},{4,3},{5,4},{6,5},{7,6},{8,7},{9,8},{10,9... | collective-permute-start | bytes 3225608 | tf_op jit(solution)/shard_map/ppermute | solution.py:29
  85.3 2.3 collective-permute-done.10
  87.6 22.2 %collective-permute-start.11 = (bf16[3,2240,80]{1,2,0:T(8,128)(2,1)S(1)}, bf16[3,2240,80]{1,2,0:T(8,128)(2,1)S(1)}, u32[]{:S(2)}, u32[]{:S(2)}) collective-permute-start(bf16[3,2240,80]{1,2,0:T(8,128)(2,1)S(1)} %collective-permute-done.10), channel_id=1, source_target_pairs={{0,15},{1,0},{2,1},{3,2},{4,3},{5,4},{6,5},{7,6},{8,7},{9,8},{10,9... | collective-permute-start | bytes 3225608 | tf_op jit(solution)/shard_map/ppermute | solution.py:29
  109.9 3.2 collective-permute-done.11
  113.0 1.0 copy-done.10
  114.0 21.5 %collective-permute-start.12 = (bf16[3,2240,80]{1,2,0:T(8,128)(2,1)S(1)}, bf16[3,2240,80]{1,2,0:T(8,128)(2,1)}, u32[]{:S(2)}, u32[]{:S(2)}) collective-permute-start(bf16[3,2240,80]{1,2,0:T(8,128)(2,1)S(1)} %collective-permute-done.11), channel_id=1, source_target_pairs={{0,15},{1,0},{2,1},{3,2},{4,3},{5,4},{6,5},{7,6},{8,7},{9,8},{10,9... | collective-permute-start | bytes 3225608 | tf_op jit(solution)/shard_map/ppermute | solution.py:29
  135.6 4.5 %collective-permute-done.12 = bf16[3,2240,80]{1,2,0:T(8,128)(2,1)} collective-permute-done((bf16[3,2240,80]{1,2,0:T(8,128)(2,1)S(1)}, bf16[3,2240,80]{1,2,0:T(8,128)(2,1)}, u32[]{:S(2)}, u32[]{:S(2)}) %collective-permute-start.12) | collective-permute-done | bytes 1075232 | tf_op jit(solution)/shard_map/ppermute | solution.py:29
  140.0 22.1 %collective-permute-start.13 = (bf16[3,2240,80]{1,2,0:T(8,128)(2,1)}, bf16[3,2240,80]{1,2,0:T(8,128)(2,1)}, u32[]{:S(2)}, u32[]{:S(2)}) collective-permute-start(bf16[3,2240,80]{1,2,0:T(8,128)(2,1)} %collective-permute-done.12), channel_id=1, source_target_pairs={{0,15},{1,0},{2,1},{3,2},{4,3},{5,4},{6,5},{7,6},{8,7},{9,8},{10,9... | collective-permute-start | bytes 3225608 | tf_op jit(solution)/shard_map/ppermute | solution.py:29
  162.2 2.6 collective-permute-done.13
  164.8 23.0 %collective-permute-start.14 = (bf16[3,2240,80]{1,2,0:T(8,128)(2,1)}, bf16[3,2240,80]{1,2,0:T(8,128)(2,1)S(1)}, u32[]{:S(2)}, u32[]{:S(2)}) collective-permute-start(bf16[3,2240,80]{1,2,0:T(8,128)(2,1)} %collective-permute-done.13), channel_id=1, source_target_pairs={{0,15},{1,0},{2,1},{3,2},{4,3},{5,4},{6,5},{7,6},{8,7},{9,8},{10,9... | collective-permute-start | bytes 3225608 | tf_op jit(solution)/shard_map/ppermute | solution.py:29
  187.9 2.4 fusion.18
  190.2 2.5 fusion.17
  192.7 1.2 fusion.16
  194.0 1.2 fusion.15
  195.2 1.2 fusion.14
  196.5 1.2 fusion.13
  197.7 1.2 fusion.12
  198.9 1.2 fusion.11
  200.1 0.1 copy-done.1
  200.1 1.2 fusion.10
  201.3 1.2 fusion.9
  202.6 1.2 fusion.8
  203.8 1.2 fusion.7
  205.0 1.2 fusion.6
  206.2 2.4 fusion.5
  208.6 2.4 fusion.4
  211.0 1.2 fusion.3
  212.1 4.8 %gather_fusion = f32[16,3,256,80]{2,3,1,0:T(8,128)} fusion(f32[16,3,256,80]{2,3,1,0:T(8,128)} %fusion.3, s32[1024]{0:T(1024)S(1)} %pad_clamp_fusion), kind=kCustom, calls=%fused_computation | custom fusion | bytes 7864384 | tf_op jit(solution)/shard_map/gather | solution.py:36
  216.9 2.1 convert_reduce_fusion
  219.1 1.4 slice.26
  220.5 1.3 fusion.41
  221.8 0.1 convert_element_type.51
  222.0 32.1 %all_gather.12 = bf16[16,40,32]{1,2,0:T(8,128)(2,1)S(1)} all-gather(bf16[1,40,32]{1,2,0:T(8,128)(2,1)S(1)} %copy.9), channel_id=1, replica_groups=mesh['groups'=2,'frame'=16] {'frame'}, dimensions={0}, use_global_device_ids=true | all-gather | bytes 43520 | tf_op jit(solution)/shard_map/all_gather | solution.py:43
  254.1 0.8 fusion.44
  254.8 37.0 %all-gather.3.cloned.1.call-done = bf16[640,32,32]{2,1,0:T(8,128)(2,1)} async-done(((bf16[40,32,32]{2,1,0:T(8,128)(2,1)}), bf16[640,32,32]{2,1,0:T(8,128)(2,1)}) %all-gather.3.cloned.1.call-update) | async-done | bytes 1310736 | tf_op jit(solution)/shard_map/all_gather | solution.py:43
  292.0 19.4 %while.12 = (s32[]{:T(128)}, f32[40,32,32]{2,1,0:T(8,128)S(1)}, f32[40,32]{1,0:T(8,128)S(1)}, s32[]{:T(128)}, bf16[16,40,32,32]{3,2,1,0:T(8,128)(2,1)}, /*index=...) while((s32[]{:T(128)}, f32[40,32,32]{2,1,0:T(8,128)S(1)}, f32[40,32]{1,0:T(8,128)S(1)}, ...), condition=%wide.region_2.3_spmd, body=%wide.region_1.2_spmd.sunk | while | flops 84485 | bytes 432775 | solution.py:57
  292.0 1.1 convert_add_fusion.4
  293.1 0.1 copy.24
  293.3 1.1 convert_add_fusion.4
  294.6 1.1 convert_add_fusion.4
  295.8 1.1 convert_add_fusion.4
  297.1 1.1 convert_add_fusion.4
  298.4 1.1 convert_add_fusion.4
  299.7 1.1 convert_add_fusion.4
  301.0 1.1 convert_add_fusion.4
  302.1 0.1 copy.24
  302.2 1.1 convert_add_fusion.4
  303.5 1.1 convert_add_fusion.4
  304.8 1.1 convert_add_fusion.4
  306.1 1.1 convert_add_fusion.4
  307.4 1.1 convert_add_fusion.4
  308.6 1.1 convert_add_fusion.4
  309.9 1.1 convert_add_fusion.4
  311.4 0.8 fusion.43
  312.1 1.3 fusion.42
  313.4 1.4 fusion.2
  314.9 1.1 copy.13
  (103 shorter events, 2.4 us)
Async XLA Ops:
  6.5 181.3 %copy-start = (bf16[1,256,2240]{1,2,0:T(8,128)(2,1)S(1)}, bf16[1,256,2240]{1,2,0:T(8,128)(2,1)}, u32[]{:S(2)}) copy-start(bf16[1,256,2240]{1,2,0:T(8,128)(2,1)} %param.4) | copy-start | bytes 3440644
  6.5 285.3 %all-gather.3.cloned.1.call-start = ((), (), s32[]{:S(2)}) async-start(), calls=%async_computation | async-start | bytes 5570560 | tf_op jit(solution)/shard_map/all_gather | solution.py:43
  6.5 12.7 %collective-permute-start = (bf16[3,2240,80]{1,2,0:T(8,128)(2,1)}, bf16[3,2240,80]{1,2,0:T(8,128)(2,1)S(1)}, u32[]{:S(2)}, u32[]{:S(2)}) collective-permute-start(bf16[3,2240,80]{1,2,0:T(8,128)(2,1)} %param.5), channel_id=1, source_target_pairs={{0,1},{1,2},{2,3},{3,4},{4,5},{5,6},{6,7},{7,8},{8,9},{9,10},{10,1... | collective-permute-start | bytes 3225608 | tf_op jit(solution)/shard_map/ppermute | solution.py:27
  19.2 17.4 %collective-permute-start.1 = (bf16[3,2240,80]{1,2,0:T(8,128)(2,1)S(1)}, bf16[3,2240,80]{1,2,0:T(8,128)(2,1)S(1)}, u32[]{:S(2)}, u32[]{:S(2)}) collective-permute-start(bf16[3,2240,80]{1,2,0:T(8,128)(2,1)S(1)} %collective-permute-done), channel_id=1, source_target_pairs={{0,1},{1,2},{2,3},{3,4},{4,5},{5,6},{6,7},{7,8},{8,9},{9,10},{10,1... | collective-permute-start | bytes 3225608 | tf_op jit(solution)/shard_map/ppermute | solution.py:27
  24.3 17.9 %collective-permute-start.8 = (bf16[3,2240,80]{1,2,0:T(8,128)(2,1)}, bf16[3,2240,80]{1,2,0:T(8,128)(2,1)S(1)}, u32[]{:S(2)}, u32[]{:S(2)}) collective-permute-start(bf16[3,2240,80]{1,2,0:T(8,128)(2,1)} %param.5), channel_id=1, source_target_pairs={{0,15},{1,0},{2,1},{3,2},{4,3},{5,4},{6,5},{7,6},{8,7},{9,8},{10,9... | collective-permute-start | bytes 3225608 | tf_op jit(solution)/shard_map/ppermute | solution.py:29
  36.6 26.5 %copy-start.2 = (bf16[3,2240,80]{1,2,0:T(8,128)(2,1)}, bf16[3,2240,80]{1,2,0:T(8,128)(2,1)S(1)}, u32[]{:S(2)}) copy-start(bf16[3,2240,80]{1,2,0:T(8,128)(2,1)S(1)} %collective-permute-done.1) | copy-start | bytes 3225604
  36.6 24.1 %collective-permute-start.2 = (bf16[3,2240,80]{1,2,0:T(8,128)(2,1)S(1)}, bf16[3,2240,80]{1,2,0:T(8,128)(2,1)S(1)}, u32[]{:S(2)}, u32[]{:S(2)}) collective-permute-start(bf16[3,2240,80]{1,2,0:T(8,128)(2,1)S(1)} %collective-permute-done.1), channel_id=1, source_target_pairs={{0,1},{1,2},{2,3},{3,4},{4,5},{5,6},{6,7},{7,8},{8,9},{9,10},{10,1... | collective-permute-start | bytes 3225608 | tf_op jit(solution)/shard_map/ppermute | solution.py:27
  42.1 21.0 %collective-permute-start.9 = (bf16[3,2240,80]{1,2,0:T(8,128)(2,1)S(1)}, bf16[3,2240,80]{1,2,0:T(8,128)(2,1)S(1)}, u32[]{:S(2)}, u32[]{:S(2)}) collective-permute-start(bf16[3,2240,80]{1,2,0:T(8,128)(2,1)S(1)} %collective-permute-done.8), channel_id=1, source_target_pairs={{0,15},{1,0},{2,1},{3,2},{4,3},{5,4},{6,5},{7,6},{8,7},{9,8},{10,9... | collective-permute-start | bytes 3225608 | tf_op jit(solution)/shard_map/ppermute | solution.py:29
  60.7 26.9 %copy-start.6 = (bf16[3,2240,80]{1,2,0:T(8,128)(2,1)}, bf16[3,2240,80]{1,2,0:T(8,128)(2,1)S(1)}, u32[]{:S(2)}) copy-start(bf16[3,2240,80]{1,2,0:T(8,128)(2,1)S(1)} %collective-permute-done.2) | copy-start | bytes 3225604
  60.7 24.5 %collective-permute-start.3 = (bf16[3,2240,80]{1,2,0:T(8,128)(2,1)S(1)}, bf16[3,2240,80]{1,2,0:T(8,128)(2,1)S(1)}, u32[]{:S(2)}, u32[]{:S(2)}) collective-permute-start(bf16[3,2240,80]{1,2,0:T(8,128)(2,1)S(1)} %collective-permute-done.2), channel_id=1, source_target_pairs={{0,1},{1,2},{2,3},{3,4},{4,5},{5,6},{6,7},{7,8},{8,9},{9,10},{10,1... | collective-permute-start | bytes 3225608 | tf_op jit(solution)/shard_map/ppermute | solution.py:27
  63.1 22.1 %copy-start.4 = (bf16[3,2240,80]{1,2,0:T(8,128)(2,1)}, bf16[3,2240,80]{1,2,0:T(8,128)(2,1)S(1)}, u32[]{:S(2)}) copy-start(bf16[3,2240,80]{1,2,0:T(8,128)(2,1)S(1)} %collective-permute-done.9) | copy-start | bytes 3225604
  63.1 24.5 %collective-permute-start.10 = (bf16[3,2240,80]{1,2,0:T(8,128)(2,1)S(1)}, bf16[3,2240,80]{1,2,0:T(8,128)(2,1)S(1)}, u32[]{:S(2)}, u32[]{:S(2)}) collective-permute-start(bf16[3,2240,80]{1,2,0:T(8,128)(2,1)S(1)} %collective-permute-done.9), channel_id=1, source_target_pairs={{0,15},{1,0},{2,1},{3,2},{4,3},{5,4},{6,5},{7,6},{8,7},{9,8},{10,9... | collective-permute-start | bytes 3225608 | tf_op jit(solution)/shard_map/ppermute | solution.py:29
  85.2 54.8 %copy-start.12 = (bf16[3,2240,80]{1,2,0:T(8,128)(2,1)}, bf16[3,2240,80]{1,2,0:T(8,128)(2,1)S(1)}, u32[]{:S(2)}) copy-start(bf16[3,2240,80]{1,2,0:T(8,128)(2,1)S(1)} %collective-permute-done.3) | copy-start | bytes 3225604
  85.2 24.6 %collective-permute-start.4 = (bf16[3,2240,80]{1,2,0:T(8,128)(2,1)S(1)}, bf16[3,2240,80]{1,2,0:T(8,128)(2,1)S(1)}, u32[]{:S(2)}, u32[]{:S(2)}) collective-permute-start(bf16[3,2240,80]{1,2,0:T(8,128)(2,1)S(1)} %collective-permute-done.3), channel_id=1, source_target_pairs={{0,1},{1,2},{2,3},{3,4},{4,5},{5,6},{6,7},{7,8},{8,9},{9,10},{10,1... | collective-permute-start | bytes 3225608 | tf_op jit(solution)/shard_map/ppermute | solution.py:27
  87.6 22.2 %copy-start.8 = (bf16[3,2240,80]{1,2,0:T(8,128)(2,1)}, bf16[3,2240,80]{1,2,0:T(8,128)(2,1)S(1)}, u32[]{:S(2)}) copy-start(bf16[3,2240,80]{1,2,0:T(8,128)(2,1)S(1)} %collective-permute-done.10) | copy-start | bytes 3225604
  87.6 25.4 %collective-permute-start.11 = (bf16[3,2240,80]{1,2,0:T(8,128)(2,1)S(1)}, bf16[3,2240,80]{1,2,0:T(8,128)(2,1)S(1)}, u32[]{:S(2)}, u32[]{:S(2)}) collective-permute-start(bf16[3,2240,80]{1,2,0:T(8,128)(2,1)S(1)} %collective-permute-done.10), channel_id=1, source_target_pairs={{0,15},{1,0},{2,1},{3,2},{4,3},{5,4},{6,5},{7,6},{8,7},{9,8},{10,9... | collective-permute-start | bytes 3225608 | tf_op jit(solution)/shard_map/ppermute | solution.py:29
  109.8 52.3 %copy-start.14 = (bf16[3,2240,80]{1,2,0:T(8,128)(2,1)}, bf16[3,2240,80]{1,2,0:T(8,128)(2,1)S(1)}, u32[]{:S(2)}) copy-start(bf16[3,2240,80]{1,2,0:T(8,128)(2,1)S(1)} %collective-permute-done.4) | copy-start | bytes 3225604
  109.8 25.7 %collective-permute-start.5 = (bf16[3,2240,80]{1,2,0:T(8,128)(2,1)S(1)}, bf16[3,2240,80]{1,2,0:T(8,128)(2,1)S(1)}, u32[]{:S(2)}, u32[]{:S(2)}) collective-permute-start(bf16[3,2240,80]{1,2,0:T(8,128)(2,1)S(1)} %collective-permute-done.4), channel_id=1, source_target_pairs={{0,1},{1,2},{2,3},{3,4},{4,5},{5,6},{6,7},{7,8},{8,9},{9,10},{10,1... | collective-permute-start | bytes 3225608 | tf_op jit(solution)/shard_map/ppermute | solution.py:27
  113.0 1.0 copy-start.10
  114.0 26.0 %collective-permute-start.12 = (bf16[3,2240,80]{1,2,0:T(8,128)(2,1)S(1)}, bf16[3,2240,80]{1,2,0:T(8,128)(2,1)}, u32[]{:S(2)}, u32[]{:S(2)}) collective-permute-start(bf16[3,2240,80]{1,2,0:T(8,128)(2,1)S(1)} %collective-permute-done.11), channel_id=1, source_target_pairs={{0,15},{1,0},{2,1},{3,2},{4,3},{5,4},{6,5},{7,6},{8,7},{9,8},{10,9... | collective-permute-start | bytes 3225608 | tf_op jit(solution)/shard_map/ppermute | solution.py:29
  135.5 26.6 %copy-start.16 = (bf16[3,2240,80]{1,2,0:T(8,128)(2,1)}, bf16[3,2240,80]{1,2,0:T(8,128)(2,1)S(1)}, u32[]{:S(2)}) copy-start(bf16[3,2240,80]{1,2,0:T(8,128)(2,1)S(1)} %collective-permute-done.5) | copy-start | bytes 3225604
  135.5 26.6 %collective-permute-start.6 = (bf16[3,2240,80]{1,2,0:T(8,128)(2,1)S(1)}, bf16[3,2240,80]{1,2,0:T(8,128)(2,1)}, u32[]{:S(2)}, u32[]{:S(2)}) collective-permute-start(bf16[3,2240,80]{1,2,0:T(8,128)(2,1)S(1)} %collective-permute-done.5), channel_id=1, source_target_pairs={{0,1},{1,2},{2,3},{3,4},{4,5},{5,6},{6,7},{7,8},{8,9},{9,10},{10,1... | collective-permute-start | bytes 3225608 | tf_op jit(solution)/shard_map/ppermute | solution.py:27
  140.0 24.8 %collective-permute-start.13 = (bf16[3,2240,80]{1,2,0:T(8,128)(2,1)}, bf16[3,2240,80]{1,2,0:T(8,128)(2,1)}, u32[]{:S(2)}, u32[]{:S(2)}) collective-permute-start(bf16[3,2240,80]{1,2,0:T(8,128)(2,1)} %collective-permute-done.12), channel_id=1, source_target_pairs={{0,15},{1,0},{2,1},{3,2},{4,3},{5,4},{6,5},{7,6},{8,7},{9,8},{10,9... | collective-permute-start | bytes 3225608 | tf_op jit(solution)/shard_map/ppermute | solution.py:29
  162.1 25.7 %collective-permute-start.7 = (bf16[3,2240,80]{1,2,0:T(8,128)(2,1)}, bf16[3,2240,80]{1,2,0:T(8,128)(2,1)}, u32[]{:S(2)}, u32[]{:S(2)}) collective-permute-start(bf16[3,2240,80]{1,2,0:T(8,128)(2,1)} %collective-permute-done.6), channel_id=1, source_target_pairs={{0,1},{1,2},{2,3},{3,4},{4,5},{5,6},{6,7},{7,8},{8,9},{9,10},{10,1... | collective-permute-start | bytes 3225608 | tf_op jit(solution)/shard_map/ppermute | solution.py:27
  164.8 46.1 %collective-permute-start.14 = (bf16[3,2240,80]{1,2,0:T(8,128)(2,1)}, bf16[3,2240,80]{1,2,0:T(8,128)(2,1)S(1)}, u32[]{:S(2)}, u32[]{:S(2)}) collective-permute-start(bf16[3,2240,80]{1,2,0:T(8,128)(2,1)} %collective-permute-done.13), channel_id=1, source_target_pairs={{0,15},{1,0},{2,1},{3,2},{4,3},{5,4},{6,5},{7,6},{8,7},{9,8},{10,9... | collective-permute-start | bytes 3225608 | tf_op jit(solution)/shard_map/ppermute | solution.py:29
  190.2 2.5 copy-start.17
  192.7 1.2 copy-start.15
  194.0 1.2 copy-start.13
  195.2 1.2 copy-start.7
  196.5 1.2 copy-start.3
  198.9 1.2 copy-start.1
  201.3 1.2 copy-start.5
  202.5 1.2 copy-start.9
  203.8 1.2 copy-start.11
  312.1 1.3 copy-start.18
Sparse Core Ops, SparseCore 0:
  221.9 69.9 all-gather.2
